TPU v7x, 32 devices: a whole 2x2x4 slice. The times are simulated.
32 devices in a mesh: seq: 16 (over z, y, core), row: 2 (over x).
Axes of the slice: x: 2, y: 2, z: 4, core: 2. Of those that a mesh axis runs over, the one named last changes fastest.
Arguments:
- layer_input: bfloat16 [2, 16384, 384], P('row', 'seq'), may hold values from -6 to 6
- segment_ids: int32 [2, 16384], P('row', 'seq'), may hold values from 0 to 63, never falling along the last dimension, each value on 1 to 512 neighbouring positions
- out_grad: bfloat16 [2, 16384, 384], P('row', 'seq'), may hold values from -6 to 6
- weights: float32 [1971840], P(('seq', 'row')), may hold values from -3 to 3
- momentum: float32 [1971840], P(('seq', 'row')), may hold values from -271.529 to 271.529
- average: float32 [1971840], P(('seq', 'row')), may hold values from -3 to 3
Outputs:
- block_output: bfloat16 [2, 16384, 384], P('row', 'seq')
- input_grad: float32 [2, 16384, 384], P('row', 'seq')
- weight_grad: float32 [1971840], P(('seq', 'row'))
- new_momentum: float32 [1971840], P(('seq', 'row'))
- new_average: float32 [1971840], P(('seq', 'row'))
- new_weights: float32 [1971840], P(('seq', 'row'))
- weight_copy: bfloat16 [1971840], P(('seq', 'row'))
Inputs may be any that keep to these rules, and one draw needn't show every extreme that they name: `segment_ids`: ids never fall along a row; every document holds 1 to 512 tokens and one of each row holds exactly 512.
All inputs are finite; a program needn't handle non-finite values.
Results may differ from a plain program's by a relative error of at most 0.012.
The roundings to bfloat16 on the way count: a program that leaves them out, or rounds other values in their place, can miss the bound.
Values may be sent and summed in bfloat16 or wider, within the bound.
A program may use at most 128 MiB of HBM per device.

v0:
```python
import math

import jax
import jax.numpy as jnp
from jax import lax
from jax.sharding import PartitionSpec as P

D = 384
HEADS = 6
HEAD_DIM = 64
FF = 1536
SPAN = 256
QBLOCK = 512


TOP_PRECISION = lax.Precision.HIGHEST
EPSILON = 1e-07


def with_halo(cells, sides, width):
    for axis, dim in sides:
        count = lax.axis_size(axis)
        ends = count - 1
        head = lax.slice_in_dim(cells, 0, width, axis=dim)
        tail = lax.slice_in_dim(cells, cells.shape[dim] - width, cells.shape[dim], axis=dim)
        cells = jnp.concatenate(
            [
                lax.ppermute(tail, axis, [(i, (i + 1) % count) for i in range(ends)]),
                cells,
                lax.ppermute(head, axis, [((i + 1) % count, i) for i in range(ends)]),
            ],
            axis=dim,
        )
    return cells


def shifted(block, axis, distance):
    devices = range(lax.axis_size(axis))
    route = [(i - distance, i) for i in devices if i - distance in devices]
    return lax.ppermute(block, axis, route)


def layer_pieces():
    return [
        ("query_w", (D, D)),
        ("key_w", (D, D)),
        ("value_w", (D, D)),
        ("output_w", (D, D)),
        ("up_w", (D, FF)),
        ("down_w", (FF, D)),
        ("query_b", (D,)),
        ("key_b", (D,)),
        ("value_b", (D,)),
        ("output_b", (D,)),
        ("attn_gain", (D,)),
        ("attn_shift", (D,)),
        ("up_bias", (FF,)),
        ("down_bias", (D,)),
        ("ffn_gain", (D,)),
        ("ffn_shift", (D,)),
    ]


def shared_pieces():
    return (("rel_table", (2 * SPAN, D)), ("rel_gain", (D,)), ("rel_shift", (D,)))


def unpack(flat_params):
    offset = 0
    weights_of = {}
    for piece_name, extent in layer_pieces():
        amount = math.prod(extent)
        weights_of[piece_name] = flat_params[offset : offset + amount].reshape(extent)
        offset += amount
    layers_list = [weights_of]
    shared = {}
    for piece_name, extent in shared_pieces():
        amount = math.prod(extent)
        shared[piece_name] = flat_params[offset : offset + amount].reshape(extent)
        offset += amount
    return (layers_list, shared)


def pack(layer_grads, shared_grads, total_length):
    pieces_out = []
    for grads_of in layer_grads:
        for piece_name, extent in layer_pieces():
            pieces_out.append(grads_of[piece_name].reshape(-1))
    for piece_name, extent in shared_pieces():
        pieces_out.append(shared_grads[piece_name].reshape(-1))
    used = sum((piece.shape[0] for piece in pieces_out))
    if total_length > used:
        pieces_out.append(jnp.zeros((total_length - used,), jnp.float32))
    return jnp.concatenate(pieces_out)


def layer_norm(values, gain, shift):
    centered = values - jnp.mean(values, axis=-1, keepdims=True)
    variance = jnp.mean(centered * centered, axis=-1, keepdims=True)
    return centered * lax.rsqrt(variance + EPSILON) * gain + shift


def norm_grads(values, gain, shift, upstream):
    outputs, pullback = jax.vjp(layer_norm, values, gain, shift)
    return pullback(upstream)


def gelu_exact(values):
    return jax.nn.gelu(values, approximate=False)


def matmul(left, right):
    return jnp.dot(left, right, preferred_element_type=jnp.float32)


def matmul_tn(left, right):
    return lax.dot_general(
        left, right, (((0,), (0,)), ((), ())), preferred_element_type=jnp.float32
    )


def matmul_nt(left, right):
    return lax.dot_general(
        left, right, (((1,), (1,)), ((), ())), preferred_element_type=jnp.float32
    )


def sheared_row_shift(matrix):
    rows_count, width = matrix.shape
    padded = jnp.pad(matrix, ((0, 0), (0, rows_count)))
    flattened = padded.reshape(-1)[: rows_count * (width + rows_count - 1)]
    return flattened.reshape(rows_count, width + rows_count - 1)


def unshear_rows(matrix, width):
    rows_count, length = matrix.shape
    flattened = jnp.pad(matrix.reshape(-1), (0, rows_count))
    return flattened.reshape(rows_count, length + 1)[:, :width]


def heads_first(matrix):
    rows_count = matrix.shape[0]
    return matrix.reshape(rows_count, HEADS, HEAD_DIM).transpose(1, 0, 2)


def heads_last(stacked):
    heads_count, rows_count, depth = stacked.shape
    return stacked.transpose(1, 0, 2).reshape(rows_count, heads_count * depth)


def block_mask(seg_ext, offset, query_rows, key_rows):
    seg_query = lax.dynamic_slice_in_dim(seg_ext, offset + SPAN, query_rows)
    seg_key = lax.dynamic_slice_in_dim(seg_ext, offset, key_rows)
    distance = lax.broadcasted_iota(jnp.int32, (query_rows, key_rows), 1) - lax.broadcasted_iota(
        jnp.int32, (query_rows, key_rows), 0
    )
    return (distance >= 0) & (distance <= 2 * SPAN) & (seg_query[:, None] == seg_key[None, :])


def head_scores(query_h, key_h, pos_key_h, pos_query_h):
    double_span = pos_key_h.shape[0] - 1
    query_rows = query_h.shape[0]
    content = matmul_nt(query_h, key_h)
    target_position = sheared_row_shift(matmul_nt(query_h, pos_key_h)[:, ::-1])
    source_position = sheared_row_shift(matmul_nt(key_h, pos_query_h))[
        :, double_span : double_span + query_rows
    ].T
    return (content + target_position + source_position) * (1.0 / math.sqrt(3.0 * query_h.shape[1]))


def head_forward(query_h, key_h, value_h, pos_key_h, pos_query_h, mask):
    scores = head_scores(query_h, key_h, pos_key_h, pos_query_h)
    masked = jnp.where(mask, scores, -1e30)
    top = jnp.max(masked, axis=1, keepdims=True)
    expv = jnp.exp(masked - top)
    total = jnp.sum(expv, axis=1, keepdims=True)
    probs = (expv / total).astype(jnp.bfloat16)
    return (matmul(probs, value_h), (top + jnp.log(total))[:, 0])


def head_backward(query_h, key_h, value_h, pos_key_h, pos_query_h, lse_h, dctx_h, mask):
    double_span = pos_key_h.shape[0] - 1
    query_rows = query_h.shape[0]
    key_rows = key_h.shape[0]
    scale = 1.0 / math.sqrt(3.0 * query_h.shape[1])
    scores = head_scores(query_h, key_h, pos_key_h, pos_query_h)
    probs = jnp.where(mask, jnp.exp(scores - lse_h[:, None]), 0.0)
    dprob = matmul_nt(dctx_h, value_h)
    dvalue = matmul_tn(probs.astype(jnp.bfloat16), dctx_h)
    inner = jnp.sum(dprob * probs, axis=1, keepdims=True)
    graw = (scale * probs * (dprob - inner)).astype(jnp.bfloat16)
    dquery = matmul(graw, key_h)
    dkey = matmul_tn(graw, query_h)
    dcpos = unshear_rows(graw, double_span + 1)[:, ::-1]
    dquery = dquery + matmul(dcpos, pos_key_h)
    dpos_key = matmul_tn(dcpos, query_h)
    padded = jnp.pad(graw.T, ((0, 0), (double_span, key_rows - query_rows)))
    dppos = unshear_rows(padded, double_span + 1)
    dkey = dkey + matmul(dppos, pos_query_h)
    dpos_query = matmul_tn(dppos, key_h)
    return (dquery, dkey, dvalue, dpos_key, dpos_query)


def attention_forward(query_low, kv_ext, seg_ext, position_key_extended, position_query_flipped):
    tokens_here = query_low.shape[0]
    query_rows = QBLOCK
    key_rows = QBLOCK + 2 * SPAN
    pos_key_heads = heads_first(position_key_extended)
    pos_query_heads = heads_first(position_query_flipped)

    def one_block(block_index):
        offset = block_index * query_rows
        query_block_rows = heads_first(lax.dynamic_slice_in_dim(query_low, offset, query_rows, 0))
        key_block_rows = heads_first(lax.dynamic_slice_in_dim(kv_ext[0], offset, key_rows, 0))
        value_blk = heads_first(lax.dynamic_slice_in_dim(kv_ext[1], offset, key_rows, 0))
        mask = block_mask(seg_ext, offset, query_rows, key_rows)
        context, lse_blk = lax.map(
            lambda head_parts: head_forward(*head_parts, mask),
            (query_block_rows, key_block_rows, value_blk, pos_key_heads, pos_query_heads),
        )
        return (heads_last(context), lse_blk)

    contexts, lses = lax.map(one_block, jnp.arange(tokens_here // query_rows, dtype=jnp.int32))
    return (contexts.reshape(tokens_here, -1), lses)


def attention_backward(
    query_low, kv_ext, seg_ext, position_key_extended, position_query_flipped, lses, dctx_low
):
    tokens_here = query_low.shape[0]
    width = query_low.shape[1]
    query_rows = QBLOCK
    key_rows = QBLOCK + 2 * SPAN
    pos_key_heads = heads_first(position_key_extended)
    pos_query_heads = heads_first(position_query_flipped)

    def one_block(carry, block_index):
        dkey_acc, dvalue_acc, dpk_acc, dpq_acc = carry
        offset = block_index * query_rows
        query_block_rows = heads_first(lax.dynamic_slice_in_dim(query_low, offset, query_rows, 0))
        key_block_rows = heads_first(lax.dynamic_slice_in_dim(kv_ext[0], offset, key_rows, 0))
        value_blk = heads_first(lax.dynamic_slice_in_dim(kv_ext[1], offset, key_rows, 0))
        dctx_blk = heads_first(lax.dynamic_slice_in_dim(dctx_low, offset, query_rows, 0))
        mask = block_mask(seg_ext, offset, query_rows, key_rows)
        dquery, dkey, dvalue, dpos_key, dpos_query = lax.map(
            lambda head_parts: head_backward(*head_parts, mask),
            (
                query_block_rows,
                key_block_rows,
                value_blk,
                pos_key_heads,
                pos_query_heads,
                lses[block_index],
                dctx_blk,
            ),
        )
        key_window = lax.dynamic_slice_in_dim(dkey_acc, offset, key_rows, 0)
        dkey_acc = lax.dynamic_update_slice_in_dim(
            dkey_acc, key_window + heads_last(dkey), offset, 0
        )
        value_window = lax.dynamic_slice_in_dim(dvalue_acc, offset, key_rows, 0)
        dvalue_acc = lax.dynamic_update_slice_in_dim(
            dvalue_acc, value_window + heads_last(dvalue), offset, 0
        )
        carry_out = (
            dkey_acc,
            dvalue_acc,
            dpk_acc + heads_last(dpos_key),
            dpq_acc + heads_last(dpos_query),
        )
        return (carry_out, heads_last(dquery))

    initial = (
        jnp.zeros((tokens_here + 2 * SPAN, width), jnp.float32),
        jnp.zeros((tokens_here + 2 * SPAN, width), jnp.float32),
        jnp.zeros((2 * SPAN + 1, width), jnp.float32),
        jnp.zeros((2 * SPAN + 1, width), jnp.float32),
    )
    sums, dquery_blocks = lax.scan(
        one_block, initial, jnp.arange(tokens_here // query_rows, dtype=jnp.int32)
    )
    return (dquery_blocks.reshape(tokens_here, width),) + sums


def layer_forward(hidden, weights_of, pos_low, seg_ext):
    x_low = hidden.astype(jnp.bfloat16)
    query_low = (
        matmul(x_low, weights_of["query_w"]) + weights_of["query_b"].astype(jnp.float32)
    ).astype(jnp.bfloat16)
    key_low = (matmul(x_low, weights_of["key_w"]) + weights_of["key_b"].astype(jnp.float32)).astype(
        jnp.bfloat16
    )
    value_low = (
        matmul(x_low, weights_of["value_w"]) + weights_of["value_b"].astype(jnp.float32)
    ).astype(jnp.bfloat16)
    kv_ext = with_halo(jnp.stack([key_low, value_low]), (("seq", 1),), SPAN)
    pos_key = (
        matmul(pos_low, weights_of["key_w"]) + weights_of["key_b"].astype(jnp.float32)
    ).astype(jnp.bfloat16)
    pos_query = (
        matmul(pos_low, weights_of["query_w"]) + weights_of["query_b"].astype(jnp.float32)
    ).astype(jnp.bfloat16)
    position_key_extended = jnp.concatenate([pos_key, pos_key[-1:]], axis=0)
    position_query_flipped = jnp.concatenate([pos_query[-1:], pos_query[::-1]], axis=0)
    context, lses = attention_forward(
        query_low, kv_ext, seg_ext, position_key_extended, position_query_flipped
    )
    context_low = context.astype(jnp.bfloat16)
    first_sum = (
        hidden
        + matmul(context_low, weights_of["output_w"])
        + weights_of["output_b"].astype(jnp.float32)
    )
    middle = layer_norm(
        first_sum,
        weights_of["attn_gain"].astype(jnp.float32),
        weights_of["attn_shift"].astype(jnp.float32),
    )
    middle_low = middle.astype(jnp.bfloat16)
    up_proj = matmul(middle_low, weights_of["up_w"]) + weights_of["up_bias"].astype(jnp.float32)
    act_low = gelu_exact(up_proj).astype(jnp.bfloat16)
    second_sum = (
        middle + matmul(act_low, weights_of["down_w"]) + weights_of["down_bias"].astype(jnp.float32)
    )
    output = layer_norm(
        second_sum,
        weights_of["ffn_gain"].astype(jnp.float32),
        weights_of["ffn_shift"].astype(jnp.float32),
    )
    saved = {
        "x_low": x_low,
        "query_low": query_low,
        "kv_ext": kv_ext,
        "pos_key_ext": position_key_extended,
        "pos_query_flip": position_query_flipped,
        "lses": lses,
        "context_low": context_low,
        "first_sum": first_sum,
        "middle_low": middle_low,
        "up_proj": up_proj,
        "act_low": act_low,
        "second_sum": second_sum,
    }
    return (output, saved)


def layer_backward(saved, weights_of, pos_low, seg_ext, grad_out):
    grads_of = {}
    tokens_here = saved["x_low"].shape[0]
    second_grad, grads_of["ffn_gain"], grads_of["ffn_shift"] = norm_grads(
        saved["second_sum"],
        weights_of["ffn_gain"].astype(jnp.float32),
        weights_of["ffn_shift"].astype(jnp.float32),
        grad_out,
    )
    down_grad = second_grad.astype(jnp.bfloat16)
    grads_of["down_w"] = matmul_tn(saved["act_low"], down_grad)
    grads_of["down_bias"] = jnp.sum(down_grad.astype(jnp.float32), axis=0)
    act_grad = matmul_nt(down_grad, weights_of["down_w"])
    up_grad = jax.vjp(gelu_exact, saved["up_proj"])[1](act_grad)[0].astype(jnp.bfloat16)
    grads_of["up_w"] = matmul_tn(saved["middle_low"], up_grad)
    grads_of["up_bias"] = jnp.sum(up_grad.astype(jnp.float32), axis=0)
    middle_grad = second_grad + matmul_nt(up_grad, weights_of["up_w"])
    first_grad, grads_of["attn_gain"], grads_of["attn_shift"] = norm_grads(
        saved["first_sum"],
        weights_of["attn_gain"].astype(jnp.float32),
        weights_of["attn_shift"].astype(jnp.float32),
        middle_grad,
    )
    attn_grad = first_grad.astype(jnp.bfloat16)
    grads_of["output_w"] = matmul_tn(saved["context_low"], attn_grad)
    grads_of["output_b"] = jnp.sum(attn_grad.astype(jnp.float32), axis=0)
    context_grad = matmul_nt(attn_grad, weights_of["output_w"]).astype(jnp.bfloat16)
    dquery, dkey_ext, dvalue_ext, dpk_ext, dpq_flip = attention_backward(
        saved["query_low"],
        saved["kv_ext"],
        seg_ext,
        saved["pos_key_ext"],
        saved["pos_query_flip"],
        saved["lses"],
        context_grad,
    )
    left_rim = jnp.stack([dkey_ext[:SPAN], dvalue_ext[:SPAN]])
    right_rim = jnp.stack([dkey_ext[SPAN + tokens_here :], dvalue_ext[SPAN + tokens_here :]])
    from_next = shifted(left_rim.astype(jnp.bfloat16), "seq", -1).astype(left_rim.dtype)
    from_prev = shifted(right_rim.astype(jnp.bfloat16), "seq", 1).astype(right_rim.dtype)
    head_pad = ((0, tokens_here - SPAN), (0, 0))
    tail_pad = ((tokens_here - SPAN, 0), (0, 0))
    dkey = (
        dkey_ext[SPAN : SPAN + tokens_here]
        + jnp.pad(from_prev[0], head_pad)
        + jnp.pad(from_next[0], tail_pad)
    )
    dvalue = (
        dvalue_ext[SPAN : SPAN + tokens_here]
        + jnp.pad(from_prev[1], head_pad)
        + jnp.pad(from_next[1], tail_pad)
    )
    dquery_low = dquery.astype(jnp.bfloat16)
    dkey_low = dkey.astype(jnp.bfloat16)
    dvalue_low = dvalue.astype(jnp.bfloat16)
    double_span = 2 * SPAN
    dpos_key = jnp.concatenate(
        [
            dpk_ext[: double_span - 1],
            dpk_ext[double_span - 1 : double_span] + dpk_ext[double_span:],
        ],
        axis=0,
    )
    reversed_rows = dpq_flip[1:][::-1]
    dpos_query = jnp.concatenate([reversed_rows[:-1], reversed_rows[-1:] + dpq_flip[:1]], axis=0)
    pos_wide = pos_low.astype(jnp.float32)
    key_wide = weights_of["key_w"].astype(jnp.float32)
    query_wide = weights_of["query_w"].astype(jnp.float32)
    x_low = saved["x_low"]
    grads_of["query_w"] = matmul_tn(x_low, dquery_low) + jnp.dot(
        pos_wide.T, dpos_query, precision=TOP_PRECISION
    )
    grads_of["key_w"] = matmul_tn(x_low, dkey_low) + jnp.dot(
        pos_wide.T, dpos_key, precision=TOP_PRECISION
    )
    grads_of["value_w"] = matmul_tn(x_low, dvalue_low)
    grads_of["query_b"] = jnp.sum(dquery_low.astype(jnp.float32), axis=0) + jnp.sum(
        dpos_query, axis=0
    )
    grads_of["key_b"] = jnp.sum(dkey_low.astype(jnp.float32), axis=0) + jnp.sum(dpos_key, axis=0)
    grads_of["value_b"] = jnp.sum(dvalue_low.astype(jnp.float32), axis=0)
    dpos = jnp.dot(dpos_key, key_wide.T, precision=TOP_PRECISION) + jnp.dot(
        dpos_query, query_wide.T, precision=TOP_PRECISION
    )
    grad_in = (
        first_grad
        + matmul_nt(dquery_low, weights_of["query_w"])
        + matmul_nt(dkey_low, weights_of["key_w"])
        + matmul_nt(dvalue_low, weights_of["value_w"])
    )
    return (grad_in, grads_of, dpos)


def on_device(layer_input, segment_ids, out_grad, weights, momentum, average):
    tokens_here = layer_input.shape[1]
    hidden = layer_input[0].astype(jnp.float32)
    seg_ext = with_halo(segment_ids[0] + 1, (("seq", 0),), SPAN)
    weights_low = weights.astype(jnp.bfloat16)
    gathered = lax.all_gather(weights_low, ("seq", "row"), axis=0, tiled=True)
    total_length = gathered.shape[0]
    layers_list, shared = unpack(gathered)
    table_wide = shared["rel_table"].astype(jnp.float32)
    table_gain = shared["rel_gain"].astype(jnp.float32)
    table_shift = shared["rel_shift"].astype(jnp.float32)
    pos_low = layer_norm(table_wide, table_gain, table_shift).astype(jnp.bfloat16)
    saved_list = []
    for weights_of in layers_list:
        hidden, saved = layer_forward(hidden, weights_of, pos_low, seg_ext)
        saved_list.append(saved)
    block_output = hidden.astype(jnp.bfloat16)
    regathered = lax.all_gather(weights_low, ("seq", "row"), axis=0, tiled=True)
    back_layers, unused_shared = unpack(regathered)
    grad_hidden = out_grad[0].astype(jnp.float32)
    grad_hidden, grads_of, dpos = layer_backward(
        saved_list[0], back_layers[0], pos_low, seg_ext, grad_hidden
    )
    grads_reversed = [grads_of]
    shared_grads = {}
    shared_grads["rel_table"], shared_grads["rel_gain"], shared_grads["rel_shift"] = norm_grads(
        table_wide, table_gain, table_shift, dpos
    )
    grad_flat = pack(grads_reversed[::-1], shared_grads, total_length)
    weight_grad = lax.psum_scatter(grad_flat, ("seq", "row"), scatter_dimension=0, tiled=True)
    all_tokens = tokens_here * lax.axis_size("seq") * layer_input.shape[0] * lax.axis_size("row")
    rate = 0.1 / math.sqrt(all_tokens)
    new_momentum = 0.5 * momentum + weight_grad
    new_weights = weights - rate * (weight_grad + 0.5 * new_momentum)
    new_average = 0.5 * average + 0.5 * new_weights
    return (
        block_output[None],
        grad_hidden[None],
        weight_grad,
        new_momentum,
        new_average,
        new_weights,
        new_weights.astype(jnp.bfloat16),
    )


def solution(mesh):
    placed = (
        P("row", "seq", None),
        P("row", "seq"),
        P("row", "seq", None),
        P(("seq", "row")),
        P(("seq", "row")),
        P(("seq", "row")),
    )
    return jax.shard_map(
        on_device,
        mesh=mesh,
        in_specs=placed,
        out_specs=(
            P("row", "seq", None),
            P("row", "seq", None),
            P(("seq", "row")),
            P(("seq", "row")),
            P(("seq", "row")),
            P(("seq", "row")),
            P(("seq", "row")),
        ),
        check_vma=False,
    )
```

profile of v0, /device:TPU:0, one launch (start us, length us, event | category | flops | bytes accessed | tf_op | source)
XLA Modules:
  0.0 2243.1 jit_solution(9400288156357425016)
XLA Ops:
  20.8 136.6 %all-reduce.16.cloned.1.call-done = bf16[1971840]{0:T(1024)(128)(2,1)} async-done(((bf16[1971840]{0:T(1024)(128)(2,1)}), bf16[1971840]{0:T(1024)(128)(2,1)}) %all-reduce.16.cloned.1.call-update) | async-done | bytes 3943696
  196.0 603.3 %while.102 = (s32[]{:T(128)}, bf16[2,512,384]{2,1,0:T(8,128)(2,1)}, f32[2,6,512]{2,1,0:T(8,128)}, s32[2]{0:T(128)}, bf16[1024,384]{0,1:T(8,128)(2,1)}, /*index=5...) while((s32[]{:T(128)}, bf16[2,512,384]{2,1,0:T(8,128)(2,1)}, ...), condition=%wide.region_7.8_spmd, body=%wide.region_2.7_spmd.sunk | while | flops 243465744 | bytes 103543456 | solution.py:223
  204.7 289.8 %while.105 = (s32[]{:T(128)}, bf16[6,512,64]{1,2,0:T(8,128)(2,1)}, f32[6,512]{1,0:T(8,128)}, bf16[6,512,64]{1,2,0:T(8,128)(2,1)S(1)}, bf16[6,1024,64]{1,2,0:T(8,...) while((s32[]{:T(128)}, bf16[6,512,64]{1,2,0:T(8,128)(2,1)}, ...), condition=%wide.region_6.6_spmd.clone, body=%wide.region_3.5_spmd.clone.sunk | while | flops 243465728 | bytes 93274336 | solution.py:217
  220.3 10.2 reshape.463
  268.6 10.2 reshape.463
  316.9 10.2 reshape.463
  365.2 10.2 reshape.463
  413.5 10.2 reshape.463
  461.8 10.2 reshape.463
  506.1 289.8 %while.105 = (s32[]{:T(128)}, bf16[6,512,64]{1,2,0:T(8,128)(2,1)}, f32[6,512]{1,0:T(8,128)}, bf16[6,512,64]{1,2,0:T(8,128)(2,1)S(1)}, bf16[6,1024,64]{1,2,0:T(8,...) while((s32[]{:T(128)}, bf16[6,512,64]{1,2,0:T(8,128)(2,1)}, ...), condition=%wide.region_6.6_spmd.clone, body=%wide.region_3.5_spmd.clone.sunk | while | flops 243465728 | bytes 93274336 | solution.py:217
  521.7 10.2 reshape.463
  570.0 10.2 reshape.463
  618.3 10.2 reshape.463
  666.6 10.2 reshape.463
  714.9 10.2 reshape.463
  763.2 10.2 reshape.463
  801.9 15.3 multiply_convert_fusion.1
  846.5 1120.3 %while.104 = (s32[]{:T(128)}, f32[1536,384]{0,1:T(8,128)}, f32[1536,384]{0,1:T(8,128)}, f32[513,384]{0,1:T(8,128)}, f32[513,384]{0,1:T(8,128)}, /*index=5*/bf16[...) while((s32[]{:T(128)}, f32[1536,384]{0,1:T(8,128)}, ...), condition=%wide.region_20.21_spmd.clone, body=%wide.region_16.20_spmd.clone.sunk | while | flops 649233408 | bytes 191010800 | solution.py:279
  861.2 534.6 %while.106 = (s32[]{:T(128)}, bf16[6,512,64]{1,2,0:T(8,128)(2,1)}, f32[6,1024,64]{1,2,0:T(8,128)}, f32[6,1024,64]{1,2,0:T(8,128)}, f32[6,513,64]{1,2,0:T(8,128)}...) while((s32[]{:T(128)}, bf16[6,512,64]{1,2,0:T(8,128)(2,1)}, ...), condition=%wide.region_19.19_spmd.clone, body=%wide.region_17.18_spmd.clone.sunk | while | flops 647659008 | bytes 146137440 | solution.py:245
  877.6 10.2 reshape.456
  914.2 8.6 reverse.5
  966.7 10.2 reshape.456
  1003.3 8.6 reverse.5
  1055.8 10.2 reshape.456
  1092.5 8.6 reverse.5
  1144.9 10.2 reshape.456
  1181.5 8.6 reverse.5
  1205.4 7.3 reshape.462
  1234.0 10.2 reshape.456
  1270.7 8.6 reverse.5
  1323.1 10.2 reshape.456
  1359.7 8.6 reverse.5
  1383.6 7.3 reshape.462
  1420.4 534.6 %while.106 = (s32[]{:T(128)}, bf16[6,512,64]{1,2,0:T(8,128)(2,1)}, f32[6,1024,64]{1,2,0:T(8,128)}, f32[6,1024,64]{1,2,0:T(8,128)}, f32[6,513,64]{1,2,0:T(8,128)}...) while((s32[]{:T(128)}, bf16[6,512,64]{1,2,0:T(8,128)(2,1)}, ...), condition=%wide.region_19.19_spmd.clone, body=%wide.region_17.18_spmd.clone.sunk | while | flops 647659008 | bytes 146137440 | solution.py:245
  1436.8 10.2 reshape.456
  1473.4 8.6 reverse.5
  1525.9 10.2 reshape.456
  1562.5 8.6 reverse.5
  1615.0 10.2 reshape.456
  1651.6 8.6 reverse.5
  1675.5 7.3 reshape.462
  1704.1 10.2 reshape.456
  1740.7 8.6 reverse.5
  1793.2 10.2 reshape.456
  1829.8 8.6 reverse.5
  1882.3 10.2 reshape.456
  1918.9 8.6 reverse.5
  2061.2 172.2 %all-reduce.18.cloned.1.call-done = f32[1971840]{0:T(1024)} async-done(((f32[1971840]{0:T(1024)}), f32[1971840]{0:T(1024)}) %all-reduce.18.cloned.1.call-update) | async-done | bytes 7887376
  (1160 shorter events, 1524.0 us)
Async XLA Ops:
  7.2 150.2 %all-reduce.16.cloned.1.call-start = ((), (), s32[]{:S(2)}) async-start(), calls=%async_computation | async-start | bytes 7888896
  10.2 7.7 copy-start.55
  13.3 5.7 copy-start.16
  13.3 2220.1 %all-reduce.18.cloned.1.call-start = ((), (), s32[]{:S(2)}) async-start(), calls=%async_computation.1 | async-start | bytes 15777792
  13.4 6.8 collective-permute-start.3
  14.9 5.4 collective-permute-start.2
  18.2 139.2 %copy-start.10 = (bf16[1,1024,384]{1,2,0:T(8,128)(2,1)}, bf16[1,1024,384]{1,2,0:T(8,128)(2,1)S(1)}, u32[]{:S(2)}) copy-start(bf16[1,1024,384]{1,2,0:T(8,128)(2,1)S(1)} %copy.85) | copy-start | bytes 2359300
  161.4 28.8 %copy-start.34 = (bf16[384,384]{1,0:T(8,128)(2,1)}, bf16[384,384]{1,0:T(8,128)(2,1)S(1)}, u32[]{:S(2)}) copy-start(bf16[384,384]{1,0:T(8,128)(2,1)S(1)} %slice.279) | copy-start | bytes 884740
  182.1 9.7 collective-permute-start
  184.1 7.6 collective-permute-start.1
  801.9 15.3 copy-start.49
  801.9 15.3 copy-start.86
  861.2 11.7 copy-start
  950.3 11.7 copy-start
  1039.4 11.7 copy-start
  1128.6 11.7 copy-start
  1217.7 11.7 copy-start
  1306.8 11.7 copy-start
  1420.4 11.7 copy-start
  1509.5 11.7 copy-start
  1598.6 11.7 copy-start
  1687.7 11.7 copy-start
  1776.9 11.7 copy-start
  1865.9 11.7 copy-start
  1955.0 5.7 copy-start.2
  1966.8 8.7 copy-start.7
  1971.0 7.4 copy-start.44
  1971.0 6.8 copy-start.17
  1977.7 6.7 copy-start.18
  1978.6 5.8 copy-start.38
  1978.6 5.8 copy-start.46
  1980.2 5.7 copy-start.63
  1980.2 5.7 copy-start.66
  1993.3 22.5 %collective-permute-start.5 = (bf16[2,256,384]{1,2,0:T(8,128)(2,1)}, bf16[2,256,384]{1,2,0:T(8,128)(2,1)}, u32[]{:S(2)}, u32[]{:S(2)}) collective-permute-start(bf16[2,256,384]{1,2,0:T(8,128)(2,1)} %pad_maximum_fusion.12), channel_id=1, source_target_pairs={{2,0},{4,2},{6,4},{8,6},{10,8},{12,10},{14,12},{16,14},{18,16},{20... | collective-permute-start | bytes 1179656 | tf_op jit(solution)/shard_map/ppermute | solution.py:40
  2007.9 9.0 collective-permute-start.4
  2026.1 6.0 copy-start.40
  2027.2 5.8 copy-start.15
  2035.5 6.9 copy-start.88
  2035.5 8.1 copy-start.87
  2035.5 9.4 copy-start.82
  2035.5 10.7 copy-start.73
  2035.6 12.0 copy-start.72
  2035.6 13.3 copy-start.71
  2035.6 14.6 copy-start.31
  2035.6 16.8 copy-start.74
  2059.5 173.9 %copy-start.53 = (f32[61620]{0:T(1024)S(1)}, f32[61620]{0:T(1024)}, u32[]{:S(2)}) copy-start(f32[61620]{0:T(1024)} %param.17) | copy-start | bytes 739444
  2059.5 173.9 %copy-start.56 = (f32[61620]{0:T(1024)S(1)}, f32[61620]{0:T(1024)}, u32[]{:S(2)}) copy-start(f32[61620]{0:T(1024)} %param.18) | copy-start | bytes 739444
  2059.5 175.8 %copy-start.57 = (f32[61620]{0:T(1024)S(1)}, f32[61620]{0:T(1024)}, u32[]{:S(2)}) copy-start(f32[61620]{0:T(1024)} %param.19) | copy-start | bytes 739444
  (154 other events, 371.9 us)
Sparse Core Ops, SparseCore 0:
  13.7 143.6 all-reduce.15
  2055.0 178.3 all-reduce.17
where the time goes:
time: 2270 us; the launch traced here: 2240 us
  local copies, waits for them, and re-layouts  1440 us (63%)
  matrix products  390 us (17%)
  waiting for transfers between devices  309 us (14%)
  other arithmetic  61.4 us (3%)
    unnamed x4, waiting for transfers between devices  309 us
    reshape x48, local copies, waits for them, and re-layouts, sheared_row_shift(): flattened = padded.reshape(-1)[:rows_count * (width + rows_count - 1)]  299 us
    while x212, local copies, waits for them, and re-layouts  212 us
    reshape x48, local copies, waits for them, and re-layouts, sheared_row_shift(): return flattened.reshape(rows_count, width + rows_count - 1)  210 us
    slice x72, local copies, waits for them, and re-layouts, sheared_row_shift(): flattened = padded.reshape(-1)[:rows_count * (width + rows_count - 1)]  153 us
    dot_general x66, matrix products, matmul_nt(): lax.dot_general(left, right, (((1,), (1,)), ((), ())), preferred_element_...  131 us
    dot_general x56, matrix products, matmul(): return jnp.dot(left, right, preferred_element_type=jnp.float32)  121 us
    pad x48, local copies, waits for them, and re-layouts, sheared_row_shift(): padded = jnp.pad(matrix, ((0, 0), (0, rows_count)))  113 us
  transfers between devices with their start and end apart: 8, of which 2 were waited for; matrix products, arithmetic and copies ran while one was open for 1% of the time, Pallas kernels for 0%

commit v1 on v0

--- a/solution.py
+++ b/solution.py
@@ -1,8 +1,11 @@
+import functools
 import math
 
 import jax
 import jax.numpy as jnp
 from jax import lax
+from jax.experimental import pallas as pl
+from jax.experimental.pallas import tpu as pltpu
 from jax.sharding import PartitionSpec as P
 
 D = 384
@@ -125,161 +128,182 @@
     )
 
 
-def sheared_row_shift(matrix):
-    rows_count, width = matrix.shape
-    padded = jnp.pad(matrix, ((0, 0), (0, rows_count)))
-    flattened = padded.reshape(-1)[: rows_count * (width + rows_count - 1)]
-    return flattened.reshape(rows_count, width + rows_count - 1)
-
-
-def unshear_rows(matrix, width):
-    rows_count, length = matrix.shape
-    flattened = jnp.pad(matrix.reshape(-1), (0, rows_count))
-    return flattened.reshape(rows_count, length + 1)[:, :width]
-
-
-def heads_first(matrix):
-    rows_count = matrix.shape[0]
-    return matrix.reshape(rows_count, HEADS, HEAD_DIM).transpose(1, 0, 2)
-
-
-def heads_last(stacked):
-    heads_count, rows_count, depth = stacked.shape
-    return stacked.transpose(1, 0, 2).reshape(rows_count, heads_count * depth)
-
-
-def block_mask(seg_ext, offset, query_rows, key_rows):
-    seg_query = lax.dynamic_slice_in_dim(seg_ext, offset + SPAN, query_rows)
-    seg_key = lax.dynamic_slice_in_dim(seg_ext, offset, key_rows)
-    distance = lax.broadcasted_iota(jnp.int32, (query_rows, key_rows), 1) - lax.broadcasted_iota(
-        jnp.int32, (query_rows, key_rows), 0
-    )
-    return (distance >= 0) & (distance <= 2 * SPAN) & (seg_query[:, None] == seg_key[None, :])
-
-
-def head_scores(query_h, key_h, pos_key_h, pos_query_h):
-    double_span = pos_key_h.shape[0] - 1
-    query_rows = query_h.shape[0]
-    content = matmul_nt(query_h, key_h)
-    target_position = sheared_row_shift(matmul_nt(query_h, pos_key_h)[:, ::-1])
-    source_position = sheared_row_shift(matmul_nt(key_h, pos_query_h))[
-        :, double_span : double_span + query_rows
-    ].T
-    return (content + target_position + source_position) * (1.0 / math.sqrt(3.0 * query_h.shape[1]))
-
-
-def head_forward(query_h, key_h, value_h, pos_key_h, pos_query_h, mask):
-    scores = head_scores(query_h, key_h, pos_key_h, pos_query_h)
-    masked = jnp.where(mask, scores, -1e30)
-    top = jnp.max(masked, axis=1, keepdims=True)
-    expv = jnp.exp(masked - top)
-    total = jnp.sum(expv, axis=1, keepdims=True)
-    probs = (expv / total).astype(jnp.bfloat16)
-    return (matmul(probs, value_h), (top + jnp.log(total))[:, 0])
-
-
-def head_backward(query_h, key_h, value_h, pos_key_h, pos_query_h, lse_h, dctx_h, mask):
-    double_span = pos_key_h.shape[0] - 1
-    query_rows = query_h.shape[0]
-    key_rows = key_h.shape[0]
-    scale = 1.0 / math.sqrt(3.0 * query_h.shape[1])
-    scores = head_scores(query_h, key_h, pos_key_h, pos_query_h)
-    probs = jnp.where(mask, jnp.exp(scores - lse_h[:, None]), 0.0)
-    dprob = matmul_nt(dctx_h, value_h)
-    dvalue = matmul_tn(probs.astype(jnp.bfloat16), dctx_h)
-    inner = jnp.sum(dprob * probs, axis=1, keepdims=True)
-    graw = (scale * probs * (dprob - inner)).astype(jnp.bfloat16)
-    dquery = matmul(graw, key_h)
-    dkey = matmul_tn(graw, query_h)
-    dcpos = unshear_rows(graw, double_span + 1)[:, ::-1]
-    dquery = dquery + matmul(dcpos, pos_key_h)
-    dpos_key = matmul_tn(dcpos, query_h)
-    padded = jnp.pad(graw.T, ((0, 0), (double_span, key_rows - query_rows)))
-    dppos = unshear_rows(padded, double_span + 1)
-    dkey = dkey + matmul(dppos, pos_query_h)
-    dpos_query = matmul_tn(dppos, key_h)
-    return (dquery, dkey, dvalue, dpos_key, dpos_query)
-
-
-def attention_forward(query_low, kv_ext, seg_ext, position_key_extended, position_query_flipped):
-    tokens_here = query_low.shape[0]
-    query_rows = QBLOCK
-    key_rows = QBLOCK + 2 * SPAN
-    pos_key_heads = heads_first(position_key_extended)
-    pos_query_heads = heads_first(position_query_flipped)
-
-    def one_block(block_index):
-        offset = block_index * query_rows
-        query_block_rows = heads_first(lax.dynamic_slice_in_dim(query_low, offset, query_rows, 0))
-        key_block_rows = heads_first(lax.dynamic_slice_in_dim(kv_ext[0], offset, key_rows, 0))
-        value_blk = heads_first(lax.dynamic_slice_in_dim(kv_ext[1], offset, key_rows, 0))
-        mask = block_mask(seg_ext, offset, query_rows, key_rows)
-        context, lse_blk = lax.map(
-            lambda head_parts: head_forward(*head_parts, mask),
-            (query_block_rows, key_block_rows, value_blk, pos_key_heads, pos_query_heads),
-        )
-        return (heads_last(context), lse_blk)
-
-    contexts, lses = lax.map(one_block, jnp.arange(tokens_here // query_rows, dtype=jnp.int32))
-    return (contexts.reshape(tokens_here, -1), lses)
-
-
-def attention_backward(
-    query_low, kv_ext, seg_ext, position_key_extended, position_query_flipped, lses, dctx_low
-):
-    tokens_here = query_low.shape[0]
-    width = query_low.shape[1]
-    query_rows = QBLOCK
-    key_rows = QBLOCK + 2 * SPAN
-    pos_key_heads = heads_first(position_key_extended)
-    pos_query_heads = heads_first(position_query_flipped)
-
-    def one_block(carry, block_index):
-        dkey_acc, dvalue_acc, dpk_acc, dpq_acc = carry
-        offset = block_index * query_rows
-        query_block_rows = heads_first(lax.dynamic_slice_in_dim(query_low, offset, query_rows, 0))
-        key_block_rows = heads_first(lax.dynamic_slice_in_dim(kv_ext[0], offset, key_rows, 0))
-        value_blk = heads_first(lax.dynamic_slice_in_dim(kv_ext[1], offset, key_rows, 0))
-        dctx_blk = heads_first(lax.dynamic_slice_in_dim(dctx_low, offset, query_rows, 0))
-        mask = block_mask(seg_ext, offset, query_rows, key_rows)
-        dquery, dkey, dvalue, dpos_key, dpos_query = lax.map(
-            lambda head_parts: head_backward(*head_parts, mask),
-            (
-                query_block_rows,
-                key_block_rows,
-                value_blk,
-                pos_key_heads,
-                pos_query_heads,
-                lses[block_index],
-                dctx_blk,
-            ),
-        )
-        key_window = lax.dynamic_slice_in_dim(dkey_acc, offset, key_rows, 0)
-        dkey_acc = lax.dynamic_update_slice_in_dim(
-            dkey_acc, key_window + heads_last(dkey), offset, 0
-        )
-        value_window = lax.dynamic_slice_in_dim(dvalue_acc, offset, key_rows, 0)
-        dvalue_acc = lax.dynamic_update_slice_in_dim(
-            dvalue_acc, value_window + heads_last(dvalue), offset, 0
-        )
-        carry_out = (
-            dkey_acc,
-            dvalue_acc,
-            dpk_acc + heads_last(dpos_key),
-            dpq_acc + heads_last(dpos_query),
-        )
-        return (carry_out, heads_last(dquery))
-
-    initial = (
-        jnp.zeros((tokens_here + 2 * SPAN, width), jnp.float32),
-        jnp.zeros((tokens_here + 2 * SPAN, width), jnp.float32),
-        jnp.zeros((2 * SPAN + 1, width), jnp.float32),
-        jnp.zeros((2 * SPAN + 1, width), jnp.float32),
-    )
-    sums, dquery_blocks = lax.scan(
-        one_block, initial, jnp.arange(tokens_here // query_rows, dtype=jnp.int32)
-    )
-    return (dquery_blocks.reshape(tokens_here, width),) + sums
+NB = 5
+PAIRS = 3
+SC = 1.0/math.sqrt(3.0*HEAD_DIM)
+LOG2E = 1.4426950408889634
+bf=jnp.bfloat16; f32=jnp.float32
+NT=(((1,),(1,)),((),())); NN=(((1,),(0,)),((),())); TN=(((0,),(0,)),((),()))
+def dot(a,b,d=NN): return lax.dot_general(a,b,d,preferred_element_type=f32)
+
+def head_mask(rows, h):
+    lane=lax.broadcasted_iota(jnp.int32,(rows,128),1)
+    return (lane<64) if h==0 else (lane>=64)
+def keep(x,h):
+    return jnp.where(head_mask(x.shape[0],h), x, jnp.zeros_like(x))
+
+def skew(A):
+    return jnp.concatenate([pltpu.roll(A[8*g:8*g+8,:512],8*g+1,1,stride=1,stride_axis=0) for g in range(16)],axis=0)
+
+
+def att_fwd_body(nblk, q_ref,k_ref,v_ref,krt_ref,qrt_ref,segq_ref,segk_ref,ctx_ref,p_ref,x_scr,bias_scr):
+    row=lax.broadcasted_iota(jnp.int32,(128,128),0); lane=lax.broadcasted_iota(jnp.int32,(128,128),1)
+    eye=(row==lane).astype(bf)
+    def mk_bias(t,c):
+        off=pl.multiple_of(t*128,128)
+        sq=segq_ref[pl.ds(off,128),:]
+        for b in range(NB):
+            sk=segk_ref[0:1,pl.ds(pl.multiple_of(off+128*b,128),128)]
+            ok = sq==sk
+            if b==0: ok = ok & (lane>=row)
+            if b==NB-1: ok = ok & (lane<=row)
+            bias_scr[t,:,128*b:128*b+128]=jnp.where(ok,0.0,-1e30).astype(f32)
+        return c
+    lax.fori_loop(0,nblk,mk_bias,0)
+    def pair(p,c):
+        def keyside(J):
+            kj=k_ref[p,pl.ds(pl.multiple_of(jnp.minimum(J,nblk+3)*128,128),128),:]
+            for h in range(2):
+                C=dot(keep(kj,h),qrt_ref[p],NT)
+                R=skew(C)
+                x_scr[h,J,:,0:128]=jnp.where(lane>row,R[:,:128],C[:,512:]).astype(bf)
+                x_scr[h,J,:,128:512]=R[:,128:].astype(bf)
+                x_scr[h,J,:,512:640]=R[:,:128].astype(bf)
+        def st(J,c):
+            keyside(J); return c
+        lax.fori_loop(0,5,st,0)
+        def qblock(t,c):
+            off=pl.multiple_of(t*128,128)
+            qt=q_ref[p,pl.ds(off,128),:]
+            kw=[k_ref[p,pl.ds(pl.multiple_of(off+128*b,128),128),:] for b in range(NB)]
+            vw=v_ref[p,pl.ds(off,640),:]
+            ctx=[]
+            for h in range(2):
+                qm=keep(qt,h)
+                A=dot(qm,krt_ref[p],NT)
+                R=skew(A)
+                lhs=jnp.concatenate([qm,eye],axis=1)
+                rhs=jnp.concatenate([jnp.concatenate([kw[b],x_scr[h,t+b,:,128*(4-b):128*(5-b)]],axis=1) for b in range(NB)],axis=0)
+                S=dot(lhs,rhs,NT)
+                Y=jnp.concatenate([jnp.where(lane>row,R[:,:128],A[:,512:]),R[:,128:],R[:,:128]],axis=1)
+                S=S+Y+bias_scr[t]
+                m=jnp.max(S,axis=1,keepdims=True)
+                e=jnp.exp2((S-m)*(SC*LOG2E))
+                s=jnp.sum(e,axis=1,keepdims=True)
+                P=(e*(1.0/s)).astype(bf)
+                p_ref[p,t,h]=P
+                ctx.append(dot(P,vw,NN))
+            ctx_ref[p,pl.ds(off,128),:]=jnp.where(lane<64,ctx[0],ctx[1]).astype(bf)
+            keyside(c)
+            return c+1
+        lax.fori_loop(0,nblk,qblock,jnp.int32(5))
+        return c
+    lax.fori_loop(0,PAIRS,pair,0)
+
+def att_fwd(q,k,v,krt,qrt,segq_b,segk):
+    T=q.shape[1]; nblk=T//128
+    return pl.pallas_call(functools.partial(att_fwd_body,nblk),
+        out_shape=[jax.ShapeDtypeStruct((PAIRS,T,128),bf),jax.ShapeDtypeStruct((PAIRS,nblk,2,128,640),bf)],
+        scratch_shapes=[pltpu.VMEM((2,nblk+5,128,640),bf),pltpu.VMEM((nblk,128,640),f32)],
+        compiler_params=pltpu.CompilerParams(vmem_limit_bytes=48<<20),
+    )(q,k,v,krt,qrt,segq_b,segk)
+
+def unskew(Grev):
+    return jnp.concatenate([pltpu.roll(Grev[8*g:8*g+8],384+8*g,1,stride=1,stride_axis=0) for g in range(16)],axis=0)
+
+def unrev(x, J):
+    hi=x.astype(bf); lo=(x-hi.astype(f32)).astype(bf)
+    y=dot(J,jnp.concatenate([hi,lo],axis=1))
+    return y[:,:128]+y[:,128:]
+
+def att_bwd_body(nblk, q_ref,k_ref,v_ref,krt_ref,qrt_ref,dctx_ref,p_ref,dq_ref,dk_ref,dv_ref,dkr_ref,dqr_ref,gt_scr,dvt_scr):
+    row=lax.broadcasted_iota(jnp.int32,(128,128),0); lane=lax.broadcasted_iota(jnp.int32,(128,128),1)
+    JR=(row+lane==127).astype(bf)
+    gt_scr[...]=jnp.zeros(gt_scr.shape,bf)
+    zero=jnp.zeros((128,128),bf)
+    def pair(p,c):
+        dvt_scr[...]=jnp.zeros(dvt_scr.shape,f32)
+        dkr_ref[p]=jnp.zeros((128,640),f32)
+        dqr_ref[p]=jnp.zeros((128,640),f32)
+        def qblock(t,J0):
+            off=pl.multiple_of(t*128,128)
+            qt=q_ref[p,pl.ds(off,128),:]
+            qT=qt.T
+            qTr=dot(qT,JR).astype(bf)
+            dct=dctx_ref[p,pl.ds(off,128),:]
+            dcT=dct.T
+            kw=k_ref[p,pl.ds(off,640),:]
+            vw=v_ref[p,pl.ds(off,640),:]
+            krt=krt_ref[p]
+            dq1=[]; dq2=[]
+            for h in range(2):
+                dp=dot(keep(dct,h),vw,NT)
+                Pb=p_ref[p,t,h]
+                Pf=Pb.astype(f32)
+                w=Pf*dp
+                inner=jnp.sum(w,axis=1,keepdims=True)
+                G=(w-Pf*inner).astype(bf)
+                Gd=jnp.where(lane==row,G[:,:128],zero)
+                Gm=jnp.concatenate([jnp.where(lane>row,G[:,:128],G[:,512:]),G[:,128:512]],axis=1)
+                Gu=unskew(dot(JR,Gm)).astype(bf)
+                dq1.append(dot(jnp.concatenate([G,Gd],axis=1),jnp.concatenate([kw,krt[512:]],axis=0)))
+                dq2.append(dot(Gu,krt[:512]))
+                hs=slice(64*h,64*h+64)
+                dkr_ref[p,hs,0:512]+=dot(qTr[hs],Gu)
+                dkr_ref[p,hs,512:640]+=dot(qT[hs],Gd)
+                dvt_scr[hs,pl.ds(off,640)]+=dot(dcT[hs],Pb)
+                for b in range(NB):
+                    gt_scr[h,J0+b,:,128*(4-b):128*(5-b)]=dot(JR,G[:,128*b:128*b+128],NT).astype(bf)
+            dq=jnp.where(lane<64,dq1[0],dq1[1])+unrev(jnp.where(lane<64,dq2[0],dq2[1]),JR)
+            dq_ref[p,pl.ds(off,128),:]=(SC*dq).astype(bf)
+            return J0+1
+        lax.fori_loop(0,nblk,qblock,jnp.int32(0))
+        def kblock(J,c):
+            off=pl.multiple_of(J*128,128)
+            kj=k_ref[p,pl.ds(off,128),:]
+            kT=kj.T
+            kTr=dot(kT,JR).astype(bf)
+            qw=jnp.concatenate([q_ref[p,pl.ds(pl.multiple_of(jnp.clip(J-4+w,0,nblk-1)*128,128),128),:] for w in range(NB)],axis=0)
+            rhs=jnp.concatenate([qw,qrt_ref[p]],axis=0)
+            dks=[]
+            for h in range(2):
+                GT=gt_scr[h,J]
+                Gd=jnp.where(lane+row==127,GT[:,:128],zero)
+                Gm=jnp.concatenate([jnp.where(lane+row>127,GT[:,:128],GT[:,512:]),GT[:,128:512]],axis=1).astype(f32)
+                Gu=unskew(Gm).astype(bf)
+                Gx=jnp.concatenate([Gu,Gd],axis=1)
+                dks.append(dot(jnp.concatenate([GT,Gx],axis=1),rhs))
+                hs=slice(64*h,64*h+64)
+                dqr_ref[p,hs,:]+=dot(kTr[hs],Gx)
+            dk_ref[p,pl.ds(off,128),:]=SC*unrev(jnp.where(lane<64,dks[0],dks[1]),JR)
+            dv_ref[p,pl.ds(off,128),:]=dvt_scr[:,pl.ds(off,128)].T
+            return c
+        lax.fori_loop(0,nblk+4,kblock,0)
+        dkr_ref[p]=SC*dkr_ref[p]
+        dqr_ref[p]=SC*dqr_ref[p]
+        return c
+    lax.fori_loop(0,PAIRS,pair,0)
+
+def att_bwd(q,k,v,krt,qrt,dctx,P):
+    T=q.shape[1]; nblk=T//128; E=T+512
+    return pl.pallas_call(functools.partial(att_bwd_body,nblk),
+        out_shape=[jax.ShapeDtypeStruct((PAIRS,T,128),bf),jax.ShapeDtypeStruct((PAIRS,E,128),f32),jax.ShapeDtypeStruct((PAIRS,E,128),f32),
+          jax.ShapeDtypeStruct((PAIRS,128,640),f32),jax.ShapeDtypeStruct((PAIRS,128,640),f32)],
+        scratch_shapes=[pltpu.VMEM((2,nblk+4,128,640),bf),pltpu.VMEM((128,E),f32)],
+        compiler_params=pltpu.CompilerParams(vmem_limit_bytes=48<<20),
+    )(q,k,v,krt,qrt,dctx,P)
+
+
+def paired(a):
+    return a.reshape(a.shape[0],PAIRS,128).transpose(1,0,2)
+
+def unpaired(a):
+    return a.transpose(1,0,2).reshape(a.shape[1],D)
+
+def untable(x):
+    x=x.reshape(D,640).T
+    y=x[:512][::-1]
+    return y.at[511].add(jnp.sum(x[512:],axis=0))
 
 
 def layer_forward(hidden, weights_of, pos_low, seg_ext):
@@ -300,11 +324,13 @@
     pos_query = (
         matmul(pos_low, weights_of["query_w"]) + weights_of["query_b"].astype(jnp.float32)
     ).astype(jnp.bfloat16)
-    position_key_extended = jnp.concatenate([pos_key, pos_key[-1:]], axis=0)
-    position_query_flipped = jnp.concatenate([pos_query[-1:], pos_query[::-1]], axis=0)
-    context, lses = attention_forward(
-        query_low, kv_ext, seg_ext, position_key_extended, position_query_flipped
-    )
+    key_table = paired(jnp.concatenate([pos_key[::-1], jnp.broadcast_to(pos_key[-1:], (128, D))], axis=0))
+    query_table = paired(jnp.concatenate([pos_query[::-1], jnp.broadcast_to(pos_query[-1:], (128, D))], axis=0))
+    tokens_here = x_low.shape[0]
+    seg_rows = jnp.broadcast_to(seg_ext[SPAN : SPAN + tokens_here, None], (tokens_here, 128))
+    qp, kp, vp = paired(query_low), paired(kv_ext[0]), paired(kv_ext[1])
+    context, probs = att_fwd(qp, kp, vp, key_table, query_table, seg_rows, seg_ext[None])
+    context = unpaired(context)
     context_low = context.astype(jnp.bfloat16)
     first_sum = (
         hidden
@@ -329,11 +355,8 @@
     )
     saved = {
         "x_low": x_low,
-        "query_low": query_low,
-        "kv_ext": kv_ext,
-        "pos_key_ext": position_key_extended,
-        "pos_query_flip": position_query_flipped,
-        "lses": lses,
+        "att": (qp, kp, vp, key_table, query_table),
+        "probs": probs,
         "context_low": context_low,
         "first_sum": first_sum,
         "middle_low": middle_low,
@@ -371,15 +394,9 @@
     grads_of["output_w"] = matmul_tn(saved["context_low"], attn_grad)
     grads_of["output_b"] = jnp.sum(attn_grad.astype(jnp.float32), axis=0)
     context_grad = matmul_nt(attn_grad, weights_of["output_w"]).astype(jnp.bfloat16)
-    dquery, dkey_ext, dvalue_ext, dpk_ext, dpq_flip = attention_backward(
-        saved["query_low"],
-        saved["kv_ext"],
-        seg_ext,
-        saved["pos_key_ext"],
-        saved["pos_query_flip"],
-        saved["lses"],
-        context_grad,
-    )
+    dquery, dkey_ext, dvalue_ext, dkr, dqr = att_bwd(*saved["att"], paired(context_grad), saved["probs"])
+    dquery, dkey_ext, dvalue_ext = unpaired(dquery), unpaired(dkey_ext), unpaired(dvalue_ext)
+    dpos_key, dpos_query = untable(dkr), untable(dqr)
     left_rim = jnp.stack([dkey_ext[:SPAN], dvalue_ext[:SPAN]])
     right_rim = jnp.stack([dkey_ext[SPAN + tokens_here :], dvalue_ext[SPAN + tokens_here :]])
     from_next = shifted(left_rim.astype(jnp.bfloat16), "seq", -1).astype(left_rim.dtype)
@@ -399,16 +416,6 @@
     dquery_low = dquery.astype(jnp.bfloat16)
     dkey_low = dkey.astype(jnp.bfloat16)
     dvalue_low = dvalue.astype(jnp.bfloat16)
-    double_span = 2 * SPAN
-    dpos_key = jnp.concatenate(
-        [
-            dpk_ext[: double_span - 1],
-            dpk_ext[double_span - 1 : double_span] + dpk_ext[double_span:],
-        ],
-        axis=0,
-    )
-    reversed_rows = dpq_flip[1:][::-1]
-    dpos_query = jnp.concatenate([reversed_rows[:-1], reversed_rows[-1:] + dpq_flip[:1]], axis=0)
     pos_wide = pos_low.astype(jnp.float32)
     key_wide = weights_of["key_w"].astype(jnp.float32)
     query_wide = weights_of["query_w"].astype(jnp.float32)

time: 2270 us -> 652 us (0.29)
  local copies, waits for them, and re-layouts: 1440 us -> 108 us
  matrix products: 390 us -> 56.6 us
  Pallas kernels: 0 us -> 107 us
  other arithmetic: 61.4 us -> 34 us
    reshape x132 -> x6, local copies, waits for them, and re-layouts: 681 us -> 8.99 us  [the longest x4 6.08 us: paired(): return a.reshape(a.shape[0], PAIRS, 128).transpose(1, 0, 2)]
    while x214 -> x0, local copies, waits for them, and re-layouts: 214 us -> none
    slice x138 -> x14, local copies, waits for them, and re-layouts: 212 us -> 17.7 us  [the longest x2 5.83 us: layer_backward(): dkey_ext[SPAN:SPAN + tokens_here] + jnp.pad(from_prev[0], head_pad)]
    pad x84 -> x0, local copies, waits for them, and re-layouts: 155 us -> none  [the longest x48 113 us: sheared_row_shift(): padded = jnp.pad(matrix, ((0, 0), (0, rows_count)))]
    dot_general x66 -> x6, matrix products: 131 us -> 11.5 us  [matmul_nt(): lax.dot_general(left, right, (((1,), (1,)), ((), ())), preferred_element_...]
    pallas_call x0 -> x2, Pallas kernels: none -> 107 us  [the longest x1 66.2 us: att_bwd(): pl.pallas_call(functools.partial(att_bwd_body, nblk), out_shape=[jax.Shap...]
    dot_general x56 -> x8, matrix products: 121 us -> 22.5 us  [matmul(): return jnp.dot(left, right, preferred_element_type=jnp.float32)]
    dot_general x54 -> x6, matrix products: 97.5 us -> 14.5 us  [matmul_tn(): lax.dot_general(left, right, (((0,), (0,)), ((), ())), preferred_element_...]
  transfers between devices with their start and end apart: 8 -> 8, of which waited for: 2 -> 3; matrix products, arithmetic and copies ran while one was open for 1% -> 8% of each run, Pallas kernels for 0% -> 0%
where the time goes in v1:
time: 652 us; the launch traced here: 643 us
  waiting for transfers between devices  308 us (47%)
  local copies, waits for them, and re-layouts  108 us (17%)
  Pallas kernels  107 us (16%)
  matrix products  56.6 us (9%)
  other arithmetic  34 us (5%)
  between operations  15.7 us (2%)
  starting transfers between devices  13.6 us (2%)
    unnamed x4, waiting for transfers between devices  306 us
    pallas_call x1, Pallas kernels, att_bwd(): pl.pallas_call(functools.partial(att_bwd_body, nblk), out_shape=[jax.Shap...  66.2 us
    unnamed x200, local copies, waits for them, and re-layouts  42.7 us
    pallas_call x1, Pallas kernels, att_fwd(): pl.pallas_call(functools.partial(att_fwd_body, nblk), out_shape=[jax.Shap...  40.6 us
    dot_general x8, matrix products, matmul(): return jnp.dot(left, right, preferred_element_type=jnp.float32)  22.5 us
    dot_general x6, matrix products, matmul_tn(): lax.dot_general(left, right, (((0,), (0,)), ((), ())), preferred_element_...  14.5 us
  transfers between devices with their start and end apart: 8, of which 3 were waited for; matrix products, arithmetic and copies ran while one was open for 8% of the time, Pallas kernels for 0%

profile of v1, /device:TPU:0, one launch (start us, length us, event | category | flops | bytes accessed | tf_op | source)
XLA Modules:
  0.0 642.7 jit_solution(10777235589612248866)
XLA Ops:
  8.2 2.0 broadcast.290
  10.2 3.0 dynamic-update-slice.6
  13.4 2.5 collective-permute-start.2
  21.1 136.3 %all-reduce.9.cloned.1.call-done = bf16[1971840]{0:T(1024)(128)(2,1)} async-done(((bf16[1971840]{0:T(1024)(128)(2,1)}), bf16[1971840]{0:T(1024)(128)(2,1)}) %all-reduce.9.cloned.1.call-update) | async-done | bytes 3943696
  159.1 2.1 fusion.43
  163.5 3.9 rev.13
  171.5 2.0 copy.61
  177.6 2.2 collective-permute-start
  184.3 1.8 slice.270
  186.1 2.2 reshape.304
  194.3 2.1 copy.56
  198.9 40.6 %shard_map.117 = (bf16[3,1024,128]{2,1,0:T(8,128)(2,1)S(1)}, bf16[3,8,2,128,640]{4,3,2,1,0:T(8,128)(2,1)}) custom-call(bf16[3,1024,128]{2,1,0:T(8,128)(2,1)S(1)} %bitcast.165, bf16[3,1536,128]{2,1,0:T(8,128)(2,1)S(1)} %bitcast.163, bf16[3,1536,128]{2,1,0:T(8,128)(2,1)S(1)} %bitcast.161, bf16[3,640,128]{2,1,0:T(8,128)(2,1)S(1)} %bitcast.169, ...), custom_call_target="tpu_custom_call" | custom-call | tf_op jit(solution)/shard_map/pallas_call | solution.py:205
  241.9 2.1 fusion.48
  244.3 15.3 %multiply_convert_fusion = (bf16[1024,1536]{1,0:T(8,128)(2,1)S(1)}, f32[1024,1536]{1,0:T(8,128)S(1)}, f32[1024,1536]{1,0:T(8,128)S(1)}) fusion(f32[1536]{0:T(1024)S(1)} %copy-done.75, bf16[384,1536]{1,0:T(8,128)(2,1)S(1)} %copy-done.53, f32[1024,384]{0,1:T(8,128)S(1)} %get-tuple-element.129, f32[384]{0:T(512)S(1)} %copy-done.83, f32[384]{0:T(512)S(1)} %copy-done.68, ...), kind=kOutput, calls=%fused_computation.4 | convolution fusion | flops 1313734656 | bytes 18498560 | tf_op jit(solution)/shard_map/dot_general | solution.py:116
  259.6 1.6 fusion.49
  263.1 2.2 convert_reduce_fusion.2
  265.3 4.5 convert_reduce_fusion
  269.8 2.7 multiply_reduce_fusion
  277.2 66.2 %shard_map.118 = (bf16[3,1024,128]{2,1,0:T(8,128)(2,1)S(1)}, f32[3,1536,128]{2,1,0:T(8,128)}, f32[3,1536,128]{2,1,0:T(8,128)}, f32[3,128,640]{2,1,0:T(8,128)S(1)}, f32[3,128,640]{2,1,0:T(8,128)S(1)}) custom-call(bf16[3,1024,128]{2,1,0:T(8,128)(2,1)S(1)} %bitcast.166, bf16[3,1536,128]{2,1,0:T(8,128)(2,1)} %bitcast.164, bf16[3,1536,128]{2,1,0:T(8,128)(2,1)} %bitcast.162, ...), custom_call_target="tpu_custom_call" | custom-call | tf_op jit(solution)/shard_map/pallas_call | solution.py:289
  346.1 1.6 copy.79
  348.8 2.2 slice.337
  353.2 2.1 slice.334
  355.3 4.9 fusion.31
  362.9 2.8 fusion.52
  367.6 2.8 multiply_reduce_fusion.4
  371.9 3.1 reshape.315
  375.1 2.7 bitcast_convert_fusion
  378.9 4.8 collective-permute-start.4
  386.3 2.7 slice.324
  389.0 3.2 copy.68
  393.3 1.7 convolution_bitcast_fusion.2
  395.1 1.6 convolution_add_fusion.4
  398.9 1.9 constant_dynamic-update-slice_fusion.18
  400.8 2.7 slice.331
  403.4 3.1 copy.74
  407.4 5.3 fusion.51
  412.8 3.2 reshape.316
  423.2 2.3 convert_reduce_fusion.4
  427.2 2.1 reshape.313
  429.2 2.0 constant_dynamic-update-slice_fusion.17
  431.3 1.9 constant_dynamic-update-slice_fusion.16
  434.1 1.6 constant_dynamic-update-slice_fusion.14
  436.7 1.6 constant_dynamic-update-slice_fusion.13
  451.3 2.2 constant_dynamic-update-slice_fusion.2
  458.3 1.7 fusion.53
  461.2 1.6 copy.84
  462.9 169.9 %all-reduce.11.cloned.1.call-done = f32[1971840]{0:T(1024)} async-done(((f32[1971840]{0:T(1024)}), f32[1971840]{0:T(1024)}) %all-reduce.11.cloned.1.call-update) | async-done | bytes 7887376
  632.7 1.9 fusion.36
  (307 shorter events, 90.3 us)
Async XLA Ops:
  7.2 150.2 %all-reduce.9.cloned.1.call-start = ((), (), s32[]{:S(2)}) async-start(), calls=%async_computation | async-start | bytes 7888896
  10.2 7.0 %copy-start.57 = (bf16[1,1024,384]{2,1,0:T(8,128)(2,1)S(1)}, bf16[1,1024,384]{2,1,0:T(8,128)(2,1)}, u32[]{:S(2)}) copy-start(bf16[1,1024,384]{2,1,0:T(8,128)(2,1)} %param.12) | copy-start | bytes 2359300
  13.3 5.1 copy-start.20
  13.3 619.4 %all-reduce.11.cloned.1.call-start = ((), (), s32[]{:S(2)}) async-start(), calls=%async_computation.1 | async-start | bytes 15777792
  13.4 6.2 collective-permute-start.2
  15.9 5.2 collective-permute-start.3
  17.5 139.9 %copy-start.14 = (bf16[1,1024,384]{1,2,0:T(8,128)(2,1)}, bf16[1,1024,384]{1,2,0:T(8,128)(2,1)S(1)}, u32[]{:S(2)}) copy-start(bf16[1,1024,384]{1,2,0:T(8,128)(2,1)S(1)} %copy.63) | copy-start | bytes 2359300
  159.1 4.4 copy-start.66
  159.1 4.4 copy-start.64
  161.4 19.9 %copy-start.46 = (bf16[384,384]{1,0:T(8,128)(2,1)}, bf16[384,384]{1,0:T(8,128)(2,1)S(1)}, u32[]{:S(2)}) copy-start(bf16[384,384]{1,0:T(8,128)(2,1)S(1)} %slice.248) | copy-start | bytes 884740
  162.8 5.1 copy-start.62
  163.1 6.0 copy-start.32
  169.1 7.6 %copy-start.35 = (bf16[1,1024,384]{1,2,0:T(8,128)(2,1)}, bf16[1,1024,384]{1,2,0:T(8,128)(2,1)S(1)}, u32[]{:S(2)}) copy-start(bf16[1,1024,384]{1,2,0:T(8,128)(2,1)S(1)} %fusion.16) | copy-start | bytes 2359300
  176.0 5.1 copy-start.30
  177.6 13.4 %collective-permute-start = (bf16[2,256,384]{1,2,0:T(8,128)(2,1)}, bf16[2,256,384]{1,2,0:T(8,128)(2,1)}, u32[]{:S(2)}, u32[]{:S(2)}) collective-permute-start(bf16[2,256,384]{1,2,0:T(8,128)(2,1)} %get-tuple-element.114), channel_id=1, source_target_pairs={{0,2},{2,4},{4,6},{6,8},{8,10},{10,12},{12,14},{14,16},{16,18},{18... | collective-permute-start | bytes 1179656 | tf_op jit(solution)/shard_map/ppermute | solution.py:31
  179.8 11.2 %collective-permute-start.1 = (bf16[2,256,384]{1,2,0:T(8,128)(2,1)}, bf16[2,256,384]{1,2,0:T(8,128)(2,1)}, u32[]{:S(2)}, u32[]{:S(2)}) collective-permute-start(bf16[2,256,384]{1,2,0:T(8,128)(2,1)} %get-tuple-element.115), channel_id=1, source_target_pairs={{2,0},{4,2},{6,4},{8,6},{10,8},{12,10},{14,12},{16,14},{18,16},{20... | collective-permute-start | bytes 1179656 | tf_op jit(solution)/shard_map/ppermute | solution.py:33
  194.3 45.3 %copy-start = (bf16[1536,3,128]{2,0,1:T(8,128)(2,1)}, bf16[1536,3,128]{2,0,1:T(8,128)(2,1)S(1)}, u32[]{:S(2)}) copy-start(bf16[1536,3,128]{2,0,1:T(8,128)(2,1)S(1)} %copy.57) | copy-start | bytes 3538948
  196.4 43.1 %copy-start.1 = (bf16[1536,3,128]{2,0,1:T(8,128)(2,1)}, bf16[1536,3,128]{2,0,1:T(8,128)(2,1)S(1)}, u32[]{:S(2)}) copy-start(bf16[1536,3,128]{2,0,1:T(8,128)(2,1)S(1)} %copy.56) | copy-start | bytes 3538948
  198.9 42.9 %copy-start.42 = (bf16[384,384]{1,0:T(8,128)(2,1)S(1)}, bf16[384,384]{1,0:T(8,128)(2,1)}, u32[]{:S(2)}) copy-start(bf16[384,384]{1,0:T(8,128)(2,1)} %slice.270) | copy-start | bytes 884740
  198.9 43.0 %copy-start.71 = (f32[384]{0:T(512)S(1)}, f32[384]{0:T(512)}, u32[]{:S(2)}) copy-start(f32[384]{0:T(512)} %get-tuple-element.98) | copy-start | bytes 4612
  244.0 28.5 %copy-start.16 = (f32[1024,384]{0,1:T(8,128)}, f32[1024,384]{0,1:T(8,128)S(1)}, u32[]{:S(2)}) copy-start(f32[1024,384]{0,1:T(8,128)S(1)} %get-tuple-element.129) | copy-start | bytes 4718596
  244.3 15.3 %copy-start.54 = (bf16[1536,384]{1,0:T(8,128)(2,1)S(1)}, bf16[1536,384]{1,0:T(8,128)(2,1)}, u32[]{:S(2)}) copy-start(bf16[1536,384]{1,0:T(8,128)(2,1)} %slice.277) | copy-start | bytes 3538948
  244.3 15.3 %copy-start.84 = (f32[384]{0:T(512)S(1)}, f32[384]{0:T(512)}, u32[]{:S(2)}) copy-start(f32[384]{0:T(512)} %get-tuple-element.95) | copy-start | bytes 4612
  265.3 4.5 copy-start.58
  346.1 4.8 copy-start.9
  348.8 6.6 %copy-start.17 = (f32[1024,384]{0,1:T(8,128)S(1)}, f32[1024,384]{0,1:T(8,128)}, u32[]{:S(2)}) copy-start(f32[1024,384]{0,1:T(8,128)} %copy-done.16) | copy-start | bytes 4718596
  355.3 4.9 copy-start.25
  361.6 4.9 copy-start.39
  362.8 4.8 copy-start.13
  362.8 4.8 copy-start.47
  362.9 4.8 copy-start.63
  362.9 4.7 copy-start.65
  378.9 37.2 %collective-permute-start.4 = (bf16[2,256,384]{1,2,0:T(8,128)(2,1)}, bf16[2,256,384]{1,2,0:T(8,128)(2,1)}, u32[]{:S(2)}, u32[]{:S(2)}) collective-permute-start(bf16[2,256,384]{1,2,0:T(8,128)(2,1)} %pad_maximum_fusion.5), channel_id=1, source_target_pairs={{0,2},{2,4},{4,6},{6,8},{8,10},{10,12},{12,14},{14,16},{16,18},{18... | collective-permute-start | bytes 1179656 | tf_op jit(solution)/shard_map/ppermute | solution.py:43
  384.8 33.2 %collective-permute-start.5 = (bf16[2,256,384]{1,2,0:T(8,128)(2,1)}, bf16[2,256,384]{1,2,0:T(8,128)(2,1)}, u32[]{:S(2)}, u32[]{:S(2)}) collective-permute-start(bf16[2,256,384]{1,2,0:T(8,128)(2,1)} %pad_maximum_fusion.6), channel_id=1, source_target_pairs={{2,0},{4,2},{6,4},{8,6},{10,8},{12,10},{14,12},{16,14},{18,16},{20... | collective-permute-start | bytes 1179656 | tf_op jit(solution)/shard_map/ppermute | solution.py:43
  427.2 6.9 %copy-start.22 = (f32[589824]{0:T(1024)S(1)}, f32[589824]{0:T(1024)}, u32[]{:S(2)}) copy-start(f32[589824]{0:T(1024)} %reshape.315) | copy-start | bytes 7077892
  436.6 5.6 copy-start.78
  436.6 6.9 %copy-start.86 = (f32[384]{0:T(512)S(1)}, f32[384]{0:T(512)}, u32[]{:S(2)}) copy-start(f32[384]{0:T(512)} %get-tuple-element.66) | copy-start | bytes 4612
  436.6 8.2 %copy-start.85 = (f32[384]{0:T(512)S(1)}, f32[384]{0:T(512)}, u32[]{:S(2)}) copy-start(f32[384]{0:T(512)} %get-tuple-element.74) | copy-start | bytes 4612
  436.6 9.4 %copy-start.76 = (f32[1536]{0:T(1024)S(1)}, f32[1536]{0:T(1024)}, u32[]{:S(2)}) copy-start(f32[1536]{0:T(1024)} %get-tuple-element.134) | copy-start | bytes 18436
  436.6 10.7 %copy-start.74 = (f32[384]{0:T(512)S(1)}, f32[384]{0:T(512)}, u32[]{:S(2)}) copy-start(f32[384]{0:T(512)} %get-tuple-element.82) | copy-start | bytes 4612
  436.6 12.0 %copy-start.73 = (f32[384]{0:T(512)S(1)}, f32[384]{0:T(512)}, u32[]{:S(2)}) copy-start(f32[384]{0:T(512)} %get-tuple-element.68) | copy-start | bytes 4612
  436.6 13.3 %copy-start.72 = (f32[384]{0:T(512)S(1)}, f32[384]{0:T(512)}, u32[]{:S(2)}) copy-start(f32[384]{0:T(512)} %convert_reduce_fusion.1) | copy-start | bytes 4612
  436.7 14.6 %copy-start.34 = (f32[196608]{0:T(1024)S(1)}, f32[196608]{0:T(1024)}, u32[]{:S(2)}) copy-start(f32[196608]{0:T(1024)} %reshape.317) | copy-start | bytes 2359300
  436.7 16.7 %copy-start.80 = (f32[384]{0:T(512)S(1)}, f32[384]{0:T(512)}, u32[]{:S(2)}) copy-start(f32[384]{0:T(512)} %get-tuple-element.72) | copy-start | bytes 4612
  436.7 18.0 %copy-start.79 = (f32[384]{0:T(512)S(1)}, f32[384]{0:T(512)}, u32[]{:S(2)}) copy-start(f32[384]{0:T(512)} %get-tuple-element.75) | copy-start | bytes 4612
  461.2 171.5 %copy-start.55 = (f32[61620]{0:T(1024)S(1)}, f32[61620]{0:T(1024)}, u32[]{:S(2)}) copy-start(f32[61620]{0:T(1024)} %param.13) | copy-start | bytes 739444
  461.2 171.5 %copy-start.59 = (f32[61620]{0:T(1024)S(1)}, f32[61620]{0:T(1024)}, u32[]{:S(2)}) copy-start(f32[61620]{0:T(1024)} %param.14) | copy-start | bytes 739444
  461.2 173.4 %copy-start.60 = (f32[61620]{0:T(1024)S(1)}, f32[61620]{0:T(1024)}, u32[]{:S(2)}) copy-start(f32[61620]{0:T(1024)} %param.15) | copy-start | bytes 739444
  (49 other events, 120.2 us)
Sparse Core Ops, SparseCore 0:
  13.7 143.6 all-reduce.8
  456.1 176.5 all-reduce.10
